TPU v7x, 32 devices: a whole 2x2x4 slice. The times are simulated.
32 devices in a mesh: groups: 2 (over x), dp: 16 (over z, y, core).
Axes of the slice: x: 2, y: 2, z: 4, core: 2. Of those that a mesh axis runs over, the one named last changes fastest.
Arguments:
- hidden: bfloat16 [128, 96, 5120], P(('groups', 'dp')), parts along dimension 0
- exit_gain: float32 [5120], replicated, may hold values from 0.5 to 1.5
- exit_weight: bfloat16 [5120, 10240], P(None, 'dp')
- labels: int32 [128], P('groups'), parts along dimension 0, may hold values from 0 to 10239
- exit_ids: int32 [64], P('groups'), parts along dimension 0, may hold values from 0 to 63, as said below
- destination: int32 [128], P('groups'), parts along dimension 0, may hold values from 0 to 15, as said below
Outputs:
- exit_nll: float32 [128], P(('groups', 'dp')), parts along dimension 0
- exit_bins: float32 [128, 15], P(('groups', 'dp')), parts along dimension 0
- moved_rows: bfloat16 [64, 96, 5120], P(('groups', 'dp')), parts along dimension 0
There are 2 independent parts, one for each index of `groups`. A program takes and returns all parts, laid end to end along the dimension named above; an argument that names none is the same for every part. Nothing has to cross between parts.
Inputs may be any that keep to these rules, and one draw needn't show every extreme that they name: `exit_ids`: 32 distinct prompt ids in no particular order. A prompt's destination is its own shard (prompts p with p // 4 as shard) or a shard next to it; a prompt in exit_ids has its own shard; from one shard at most one surviving prompt goes to each neighbour, and every shard receives exactly 2 surviving prompts.
All inputs are finite; a program needn't handle non-finite values.
Results may differ from a plain program's by a relative error of at most 0.0019.
The roundings to bfloat16 on the way count: a program that leaves them out, or rounds other values in their place, can miss the bound.
Values may be sent and summed in bfloat16 or wider, within the bound.
A program may use at most 128 MiB of HBM per device.

v0:
```python
import math

import jax
import jax.numpy as jnp
from jax import lax
from jax.sharding import PartitionSpec as P

BINS = 15


epsilon = 1e-06


def merged_2(x, axis, combine):
    everything = jax.tree.map(lambda part: lax.all_gather(part, axis), x)
    initial = jax.tree.map(lambda part: part[0], everything)

    def lap(k, so_far):
        return combine(so_far, jax.tree.map(lambda part: part[k], everything))

    return lax.fori_loop(1, lax.axis_size(axis), lap, initial)


def extended(x, sides, width):
    for axis, dim in sides:
        size, length = (lax.axis_size(axis), x.shape[dim])
        up = [(i, (i + 1) % size) for i in range(size - 1)]
        down = [(j, i) for i, j in up]
        last = lax.slice_in_dim(x, length - width, length, axis=dim)
        initial = lax.slice_in_dim(x, 0, width, axis=dim)
        before = lax.ppermute(last, axis, up)
        after = lax.ppermute(initial, axis, down)
        x = jnp.concatenate([before, x, after], axis=dim)
    return x


def combine_stats(earlier, latter):
    peak_value = jnp.maximum(earlier[0], latter[0])
    exponent_sum = earlier[1] * jnp.exp(earlier[0] - peak_value) + latter[1] * jnp.exp(
        latter[0] - peak_value
    )
    return (peak_value, exponent_sum, earlier[2] + latter[2])


def shards(hidden, exit_gain, exit_weight, labels, exit_ids, destination):
    per_shard = hidden.shape[0]
    survive_slots = per_shard // 2
    shard_count = lax.axis_size("dp")
    local_shard_index = lax.axis_index("dp")
    vocab_width = exit_weight.shape[1]
    vocab_total = vocab_width * shard_count
    every_prompt = per_shard * shard_count
    final_rows = hidden[:, -1, :].astype(jnp.float32)
    mean_square = jnp.mean(final_rows * final_rows, axis=1, keepdims=True)
    normed = (final_rows * lax.rsqrt(mean_square + epsilon) * exit_gain).astype(jnp.bfloat16)
    vocab_ids = local_shard_index * vocab_width + jnp.arange(vocab_width, dtype=jnp.int32)
    logits = jnp.dot(
        lax.all_gather(normed, "dp", axis=0, tiled=True),
        exit_weight,
        preferred_element_type=jnp.float32,
    )
    peak_value = jnp.max(logits, axis=1)
    exponent_sum = jnp.sum(jnp.exp(logits - peak_value[:, None]), axis=1)
    label_match = jnp.sum(jnp.where(vocab_ids[None, :] == labels[:, None], logits, 0.0), axis=1)
    peaks = peak_value
    totals = exponent_sum
    picked = label_match
    peaks, totals, picked = (peaks, totals, picked)
    merged = merged_2((peaks, totals, picked), "dp", combine_stats)
    offset = local_shard_index * per_shard
    peak_value = lax.dynamic_slice_in_dim(merged[0], offset, per_shard, 0)
    exponent_sum = lax.dynamic_slice_in_dim(merged[1], offset, per_shard, 0)
    label_logit = lax.dynamic_slice_in_dim(merged[2], offset, per_shard, 0)
    log_total = peak_value + jnp.log(exponent_sum)
    exit_nll = log_total - label_logit
    bin_place = BINS * (1.0 + (peak_value - log_total) / math.log(vocab_total))
    centres = jnp.arange(BINS, dtype=jnp.float32) + 0.5
    exit_bins = jnp.maximum(0.0, 1.0 - jnp.abs(bin_place[:, None] - centres[None, :]))
    prompt_ids = jnp.arange(every_prompt, dtype=jnp.int32)
    leaving = jnp.any(prompt_ids[:, None] == exit_ids[None, :], axis=1)
    target = jnp.where(leaving, -1, destination)
    window = extended(hidden, (("dp", 0),), per_shard)
    positions = (local_shard_index - 1) * per_shard + jnp.arange(3 * per_shard, dtype=jnp.int32)
    inside = (positions >= 0) & (positions < every_prompt)
    targets = jnp.where(inside, jnp.take(target, jnp.clip(positions, 0, every_prompt - 1)), -1)
    matches = targets == local_shard_index
    ranking = jnp.cumsum(matches.astype(jnp.int32)) - 1
    slot_range = jnp.arange(survive_slots, dtype=jnp.int32)
    column_ids = jnp.arange(targets.shape[0], dtype=jnp.int32)
    chosen = jnp.sum(
        jnp.where(
            matches[None, :] & (ranking[None, :] == slot_range[:, None]), column_ids[None, :], 0
        ),
        axis=1,
    )
    moved_rows = jnp.take(window, chosen, axis=0)
    return (exit_nll, exit_bins, moved_rows)


def solution(mesh):
    in_specs = (
        P(("groups", "dp"), None, None),
        P(),
        P(None, "dp"),
        P("groups"),
        P("groups"),
        P("groups"),
    )
    out_specs = (P(("groups", "dp")), P(("groups", "dp"), None), P(("groups", "dp"), None, None))
    return jax.shard_map(shards, mesh=mesh, in_specs=in_specs, out_specs=out_specs, check_vma=False)
```

profile of v0, /device:TPU:0, one launch (start us, length us, event | category | flops | bytes accessed | tf_op | source)
XLA Modules:
  0.0 193.4 jit_solution(5112624900136556607)
XLA Ops:
  0.6 1.3 collective-permute-start.1
  1.9 4.9 %collective-permute-start = (bf16[4,96,5120]{2,1,0:T(8,128)(2,1)}, bf16[4,96,5120]{2,1,0:T(8,128)(2,1)}, u32[]{:S(2)}, u32[]{:S(2)}) collective-permute-start(bf16[4,96,5120]{2,1,0:T(8,128)(2,1)} %param.8), channel_id=1, source_target_pairs={{0,1},{1,2},{2,3},{3,4},{4,5},{5,6},{6,7},{7,8},{8,9},{9,10},{10,1... | collective-permute-start | bytes 11796488 | tf_op jit(solution)/shard_map/ppermute | solution.py:31
  6.9 1.0 slice_convert_fusion
  7.9 0.2 fusion.7
  8.1 0.8 fusion.10
  8.9 96.7 %all-gather.3 = bf16[16,4,5120]{2,1,0:T(4,128)(2,1)S(1)} all-gather(bf16[1,4,5120]{2,1,0:T(4,128)(2,1)S(1)} %fusion.10), channel_id=1, replica_groups=mesh['groups'=2,'dp'=16] {'dp'}, dimensions={0}, use_global_device_ids=true | all-gather | bytes 696320 | tf_op jit(solution)/shard_map/all_gather | solution.py:58
  105.6 0.1 reshape.192
  105.8 0.0 copy-start.3
  105.8 0.0 copy-start
  105.8 0.0 copy-start.1
  105.8 0.0 copy-start.2
  105.9 4.1 %fusion.17 = (f32[64]{0:T(128)S(1)}, f32[64,640]{1,0:T(8,128)S(1)}) fusion(bf16[64,5120]{1,0:T(8,128)(2,1)S(1)} %reshape.192, bf16[5120,640]{1,0:T(8,128)(2,1)} %param.10), kind=kOutput, calls=%fused_computation.52 | convolution fusion | flops 419471296 | bytes 7373056 | tf_op jit(solution)/shard_map/dot_general | solution.py:57
  110.0 0.0 copy-done.3
  110.0 0.6 dynamic-slice
  111.2 0.2 dynamic-update-slice
  111.5 0.0 copy-done
  111.5 0.2 select_reduce_fusion
  111.7 0.2 dynamic-update-slice.1
  112.0 0.2 dynamic-update-slice.2
  112.2 61.2 %all-reduce.3 = (f32[1024]{0:T(1024)S(1)}, f32[1024]{0:T(1024)S(1)}, f32[1024]{0:T(1024)S(1)}) all-reduce(f32[1024]{0:T(1024)S(1)} %dynamic-update-slice, f32[1024]{0:T(1024)S(1)} %dynamic-update-slice.1, f32[1024]{0:T(1024)S(1)} %dynamic-update-slice.2), channel_id=2, replica_groups=mesh['groups'=2,'dp'=16] {'dp'}, use_global_device_ids=true, to_apply=%add | all-reduce | flops 3072 | bytes 24576
  173.4 0.1 reshape.173
  173.5 0.1 reshape.174
  173.5 0.1 reshape.175
  173.6 0.0 copy-done.1
  173.6 0.1 fusion.11
  173.7 0.0 copy-done.2
  173.7 0.7 gather_fusion
  174.4 0.2 reduce-window.8
  174.6 0.7 while.19
  175.3 0.6 add_multiply_fusion
  175.9 0.1 fusion.12
  176.1 0.7 subtract_maximum_fusion
  176.7 0.0 collective-permute-done.1
  176.7 0.0 collective-permute-done
  176.7 10.1 %pad_maximum_fusion = bf16[12,96,5120]{2,1,0:T(8,128)(2,1)} fusion(bf16[4,96,5120]{2,1,0:T(8,128)(2,1)} %collective-permute-done.1, bf16[4,96,5120]{2,1,0:T(8,128)(2,1)} %param.8, bf16[4,96,5120]{2,1,0:T(8,128)(2,1)} %collective-permute-done), kind=kLoop, calls=%fused_computation.12 | loop fusion | flops 11796480 | bytes 23592960 | tf_op jit(solution)/shard_map/concatenate | solution.py:33
  186.8 5.0 %gather_fusion.1 = bf16[2,96,5120]{2,1,0:T(8,128)(2,1)S(1)} fusion(bf16[12,96,5120]{2,1,0:T(8,128)(2,1)} %pad_maximum_fusion, s32[1024]{0:T(1024)S(1)} %pad_clamp_fusion), kind=kCustom, calls=%fused_computation.1 | custom fusion | bytes 3932168 | tf_op jit(solution)/shard_map/jit(_take)/gather | solution.py:96
  191.9 1.5 broadcast_select_fusion
  (33 shorter events, 0.5 us)
Async XLA Ops:
  0.6 176.1 %collective-permute-start.1 = (bf16[4,96,5120]{2,1,0:T(8,128)(2,1)}, bf16[4,96,5120]{2,1,0:T(8,128)(2,1)}, u32[]{:S(2)}, u32[]{:S(2)}) collective-permute-start(bf16[4,96,5120]{2,1,0:T(8,128)(2,1)} %param.8), channel_id=1, source_target_pairs={{1,0},{2,1},{3,2},{4,3},{5,4},{6,5},{7,6},{8,7},{9,8},{10,9},{11,1... | collective-permute-start | bytes 11796488 | tf_op jit(solution)/shard_map/ppermute | solution.py:32
  1.9 174.8 %collective-permute-start = (bf16[4,96,5120]{2,1,0:T(8,128)(2,1)}, bf16[4,96,5120]{2,1,0:T(8,128)(2,1)}, u32[]{:S(2)}, u32[]{:S(2)}) collective-permute-start(bf16[4,96,5120]{2,1,0:T(8,128)(2,1)} %param.8), channel_id=1, source_target_pairs={{0,1},{1,2},{2,3},{3,4},{4,5},{5,6},{6,7},{7,8},{8,9},{9,10},{10,1... | collective-permute-start | bytes 11796488 | tf_op jit(solution)/shard_map/ppermute | solution.py:31
  105.8 4.2 %copy-start.3 = (u32[32]{0:T(128)S(1)}, u32[32]{0:T(128)}, u32[]{:S(2)}) copy-start(u32[32]{0:T(128)} %constant.113) | copy-start | bytes 388
  105.8 5.7 %copy-start = (s32[64]{0:T(128)S(1)}, s32[64]{0:T(128)}, u32[]{:S(2)}) copy-start(s32[64]{0:T(128)} %param.11) | copy-start | bytes 772
  105.8 67.8 %copy-start.1 = (s32[32]{0:T(128)S(1)}, s32[32]{0:T(128)}, u32[]{:S(2)}) copy-start(s32[32]{0:T(128)} %param.12) | copy-start | bytes 388
  105.8 67.9 %copy-start.2 = (s32[64]{0:T(128)S(1)}, s32[64]{0:T(128)}, u32[]{:S(2)}) copy-start(s32[64]{0:T(128)} %param.13) | copy-start | bytes 772
where the time goes:
time: 194 us; the launch traced here: 193 us
  blocking collectives  158 us (81%)
  other arithmetic  16 us (8%)
  local copies, waits for them, and re-layouts  7.36 us (4%)
  starting transfers between devices  6.23 us (3%)
  matrix products  4.13 us (2%)
    all_gather x1, blocking collectives, shards(): lax.all_gather(normed, 'dp', axis=0, tiled=True)  96.7 us
    unnamed x1, blocking collectives  61.2 us
    concatenate x1, other arithmetic, extended(): x = jnp.concatenate([before, x, after], axis=dim)  10.1 us
    gather x1, local copies, waits for them, and re-layouts, shards(): moved_rows = jnp.take(window, chosen, axis=0)  5.02 us
    ppermute x1, starting transfers between devices, extended(): before = lax.ppermute(last, axis, up)  4.94 us
    dot_general x1, matrix products, shards(): jnp.dot(lax.all_gather(normed, 'dp', axis=0, tiled=True), exit_weight, pr...  4.13 us
  transfers between devices with their start and end apart: 2, of which 0 were waited for; matrix products, arithmetic and copies ran while one was open for 6% of the time, Pallas kernels for 0%

commit v1 on v0

v1 whole, which is shorter than its diff:
```python
import functools
import math

import jax
import jax.numpy as jnp
from jax import lax
from jax.experimental import pallas as pl
from jax.experimental.pallas import tpu as pltpu
from jax.sharding import PartitionSpec as P

BINS = 15
EPSILON = 1e-06
PACK = 16
CHUNK = 16
MESH = pl.DeviceIdType.MESH


def partner_of(me, bit):
    return me + (1 - 2 * ((me // (1 << bit)) % 2)) * (1 << bit)


def block_of(me, mask, bits):
    for bit in range(bits):
        if mask >> bit & 1:
            me = partner_of(me, bit)
    return me


def kernel(
    n,
    per,
    hidden,
    weight,
    gain,
    label_row,
    exit_ids,
    destination,
    moved,
    result,
    held,
    weights,
    raw,
    rows,
    outgoing,
    incoming,
    staged,
    stats,
    arrived,
    load_sem,
    weight_sem,
    row_send,
    row_recv,
    big_send,
    big_recv,
    stat_send,
    stat_recv,
    out_sem,
):
    me = lax.axis_index("dp")
    bits = n.bit_length() - 1
    parts = PACK // per
    width = hidden.shape[2] // parts
    pieces = len(held)
    vocab = weight.shape[1]
    vocab_total = vocab * n

    barrier = pltpu.get_barrier_semaphore()

    def greet(k, carry):
        pl.semaphore_signal(
            barrier, inc=1, device_id={"dp": (me + k) % n}, device_id_type=MESH
        )
        return carry

    loads = {}
    order = [pieces - 1] + list(range(pieces - 1))
    for c in order:
        loads[c] = pltpu.make_async_copy(
            hidden.at[:, pl.ds(c * CHUNK, CHUNK), :], held[c], load_sem.at[c]
        )
        loads[c].start()
    lax.fori_loop(1, n, greet, 0)
    weight_copy = pltpu.make_async_copy(weight, weights, weight_sem)
    weight_copy.start()

    loads[pieces - 1].wait()
    for p in range(per):
        row = held[pieces - 1][p, CHUNK - 8 : CHUNK, :].astype(jnp.float32)[7:8, :]
        for q in range(parts):
            raw[q * per + p : q * per + p + 1, :] = row[:, q * width : (q + 1) * width]
    values = raw[...]
    squares = jnp.sum(values * values, axis=1, keepdims=True)
    squares = jnp.broadcast_to(squares, (PACK, 128))
    shift = per
    while shift < PACK:
        squares = squares + pltpu.roll(squares, shift, 0)
        shift *= 2
    scale = lax.rsqrt(squares[:, :1] / hidden.shape[2] + EPSILON)
    part_of = lax.broadcasted_iota(jnp.int32, (PACK, width), 0) // per
    gains = jnp.zeros((PACK, width), jnp.float32)
    for q in range(parts):
        gains = jnp.where(part_of == q, gain[:, q * width : (q + 1) * width], gains)
    rows[me] = (values * scale * gains).astype(jnp.bfloat16)

    pl.semaphore_wait(barrier, n - 1)

    bit_order = list(range(1, bits)) + [0]
    sent = []

    def send_stage(stage, have):
        bit = bit_order[stage]
        new = []
        for mask in have:
            j = block_of(me, mask, bits)
            to = mask ^ (1 << bit)
            if mask:
                got(mask)
            copy = pltpu.make_async_remote_copy(
                src_ref=rows.at[j],
                dst_ref=rows.at[j],
                send_sem=row_send.at[to],
                recv_sem=row_recv.at[to],
                device_id={"dp": partner_of(me, bit)},
                device_id_type=MESH,
            )
            copy.start()
            sent.append(copy)
            new.append(to)
        return have + new

    seen = set()

    def got(mask):
        if mask in seen:
            return
        seen.add(mask)
        j = block_of(me, mask, bits)
        pltpu.make_async_remote_copy(
            src_ref=rows.at[j],
            dst_ref=rows.at[j],
            send_sem=row_send.at[mask],
            recv_sem=row_recv.at[mask],
            device_id={"dp": partner_of(me, 0)},
            device_id_type=MESH,
        ).wait_recv()

    have = send_stage(0, [0])

    target = [destination[me * per + i] for i in range(per)]
    to_right = jnp.int32(0)
    to_left = jnp.int32(0)
    for i in range(1, per):
        to_right = jnp.where(target[i] == me + 1, i, to_right)
        to_left = jnp.where(target[i] == me - 1, i, to_left)
    chosen = (to_right, to_left)
    can_send = (me < n - 1, me > 0)
    can_receive = (me > 0, me < n - 1)

    def big_copy(side, c):
        other = jnp.clip(me + 1 - 2 * side, 0, n - 1)
        return pltpu.make_async_remote_copy(
            src_ref=outgoing.at[side, c],
            dst_ref=incoming.at[side, c],
            send_sem=big_send.at[side, c],
            recv_sem=big_recv.at[side, c],
            device_id={"dp": other},
            device_id_type=MESH,
        )

    for c in order:
        if c != pieces - 1:
            loads[c].wait()
        for side in range(2):
            outgoing[side, c] = held[c][chosen[side]]

            @pl.when(can_send[side])
            def _():
                big_copy(side, c).start()

    for stage in range(1, bits):
        have = send_stage(stage, have)

    count = exit_ids.shape[0]

    def lookup(k, leaving):
        e = exit_ids[k] - me * per
        return tuple(jnp.where(e == i, 1, leaving[i]) for i in range(per))

    leaving = lax.fori_loop(0, count, lookup, (jnp.int32(0),) * per)
    first = jnp.int32(0)
    last = jnp.int32(0)
    for i in range(per):
        last = jnp.where((target[i] == me) & (leaving[i] == 0), i, last)
        k = per - 1 - i
        first = jnp.where((target[k] == me) & (leaving[k] == 0), k, first)
    before = jnp.maximum(me - 1, 0) * per
    after = jnp.minimum(me + 1, n - 1) * per
    from_left = jnp.int32(0)
    from_right = jnp.int32(0)
    for i in range(per):
        from_left = jnp.where(destination[before + i] == me, 1, from_left)
        from_right = jnp.where(destination[after + i] == me, 1, from_right)
    from_left = jnp.where(me > 0, from_left, 0)
    from_right = jnp.where(me < n - 1, from_right, 0)

    weight_copy.wait()
    for mask in range(1, n):
        got(mask)
    group = min(n, 16)
    high = group * PACK
    every = label_row.shape[1]

    def block(b, carry):
        held_rows = rows[pl.ds(b * group, group)].reshape(high, width)
        row_id = lax.broadcasted_iota(jnp.int32, (high, vocab), 0)
        row_part = (row_id // per) % parts
        logits = jnp.zeros((high, vocab), jnp.float32)
        for q in range(parts):
            product = jnp.dot(
                held_rows,
                weights[q * width : (q + 1) * width, :],
                preferred_element_type=jnp.float32,
            )
            logits = jnp.where(row_part == q, product, logits)
        shift = per
        while shift < PACK:
            logits = logits + pltpu.roll(logits, shift, 0)
            shift *= 2
        peak = jnp.max(logits, axis=1, keepdims=True)
        total = jnp.sum(jnp.exp(logits - peak), axis=1, keepdims=True)
        r = lax.broadcasted_iota(jnp.int32, (high, every), 0)
        prompt = (b * group + r // PACK) * per + r % per
        column = lax.broadcasted_iota(jnp.int32, (high, every), 1)
        label = jnp.sum(
            jnp.where(column == prompt, label_row[...].astype(jnp.float32), 0.0),
            axis=1,
            keepdims=True,
        )
        ids = lax.broadcasted_iota(jnp.int32, (high, vocab), 1) + me * vocab
        picked = jnp.sum(
            jnp.where(ids.astype(jnp.float32) == label, logits, 0.0), axis=1, keepdims=True
        )
        lane = lax.broadcasted_iota(jnp.int32, (high, 128), 1)
        packed = jnp.where(lane == 0, peak, jnp.where(lane == 1, total, picked))
        stats[pl.ds(b * group, group)] = packed.reshape(group, PACK, 128)[:, PACK - 8 :, :]
        return carry

    if n == group:
        block(0, 0)
    else:
        lax.fori_loop(0, n // group, block, 0)

    def stat_copy(k, source):
        other = (me + k) % n
        return pltpu.make_async_remote_copy(
            src_ref=stats.at[other],
            dst_ref=arrived.at[source],
            send_sem=stat_send.at[k],
            recv_sem=stat_recv.at[k],
            device_id={"dp": other},
            device_id_type=MESH,
        )

    def stat_start(k, carry):
        stat_copy(k, me).start()
        return carry

    lax.fori_loop(1, n, stat_start, 0)
    arrived[me] = stats[me]

    gets = (from_left, from_right)
    keeps = (first, last)
    for c in order:
        for side in range(2):

            @pl.when(can_receive[side])
            def _():
                big_copy(side, c).wait_recv()

            own = held[c][keeps[side]]
            staged[side, c] = jnp.where(gets[side] > 0, incoming[side, c], own)
            pltpu.make_async_copy(
                staged.at[side, c],
                moved.at[side, pl.ds(c * CHUNK, CHUNK), :],
                out_sem.at[side, c],
            ).start()

    def stat_wait(k, carry):
        stat_copy(k, (me + n - k) % n).wait_recv()
        return carry

    lax.fori_loop(1, n, stat_wait, 0)
    everything = arrived[...]
    peaks = everything[:, :, 0:1]
    peak = jnp.max(peaks, axis=0)
    total = jnp.sum(everything[:, :, 1:2] * jnp.exp(peaks - peak[None]), axis=0)
    picked = jnp.sum(everything[:, :, 2:3], axis=0)
    log_total = peak + jnp.log(total)
    nll = log_total - picked
    place = BINS * (1.0 + (peak - log_total) / math.log(vocab_total))
    lane = lax.broadcasted_iota(jnp.int32, (8, 128), 1)
    centre = lane.astype(jnp.float32) + 0.5
    bins = jnp.maximum(0.0, 1.0 - jnp.abs(place - centre))
    result[...] = jnp.where(lane < BINS, bins, nll)

    for c in order:
        for side in range(2):
            pltpu.make_async_copy(
                staged.at[side, c],
                moved.at[side, pl.ds(c * CHUNK, CHUNK), :],
                out_sem.at[side, c],
            ).wait()

            @pl.when(can_send[side])
            def _():
                big_copy(side, c).wait_send()

    for copy in sent:
        copy.wait_send()

    def stat_done(k, carry):
        stat_copy(k, me).wait_send()
        return carry

    lax.fori_loop(1, n, stat_done, 0)


def shards(hidden, exit_gain, exit_weight, labels, exit_ids, destination):
    n = lax.axis_size("dp")
    per, length, depth = hidden.shape
    vocab = exit_weight.shape[1]
    pieces = length // CHUNK
    slots = per // 2
    width = depth // (PACK // per)
    hbm = pl.BlockSpec(memory_space=pl.ANY)
    vmem = pl.BlockSpec(memory_space=pltpu.VMEM)
    smem = pl.BlockSpec(memory_space=pltpu.SMEM)
    bf16 = jnp.bfloat16
    moved, result = pl.pallas_call(
        lambda *refs: kernel(n, per, *refs),
        out_shape=(
            jax.ShapeDtypeStruct((slots, length, depth), bf16),
            jax.ShapeDtypeStruct((8, 128), jnp.float32),
        ),
        in_specs=[hbm, hbm, vmem, vmem, smem, smem],
        out_specs=(hbm, vmem),
        scratch_shapes=[
            [pltpu.VMEM((per, CHUNK, depth), bf16) for _ in range(pieces)],
            pltpu.VMEM((depth, vocab), bf16),
            pltpu.VMEM((PACK, width), jnp.float32),
            pltpu.VMEM((n, PACK, width), bf16),
            pltpu.VMEM((2, pieces, CHUNK, depth), bf16),
            pltpu.VMEM((2, pieces, CHUNK, depth), bf16),
            pltpu.VMEM((2, pieces, CHUNK, depth), bf16),
            pltpu.VMEM((n, 8, 128), jnp.float32),
            pltpu.VMEM((n, 8, 128), jnp.float32),
            pltpu.SemaphoreType.DMA((pieces,)),
            pltpu.SemaphoreType.DMA,
            pltpu.SemaphoreType.DMA((n,)),
            pltpu.SemaphoreType.DMA((n,)),
            pltpu.SemaphoreType.DMA((2, pieces)),
            pltpu.SemaphoreType.DMA((2, pieces)),
            pltpu.SemaphoreType.DMA((n,)),
            pltpu.SemaphoreType.DMA((n,)),
            pltpu.SemaphoreType.DMA((2, pieces)),
        ],
        compiler_params=pltpu.CompilerParams(
            collective_id=0, has_side_effects=True, vmem_limit_bytes=56 * 1024 * 1024
        ),
    )(
        hidden,
        exit_weight,
        exit_gain.reshape(1, depth),
        labels.reshape(1, -1),
        exit_ids,
        destination,
    )
    valid = result[8 - per :]
    return valid[:, 127], valid[:, :BINS], moved


def solution(mesh):
    in_specs = (
        P(("groups", "dp"), None, None),
        P(),
        P(None, "dp"),
        P("groups"),
        P("groups"),
        P("groups"),
    )
    out_specs = (P(("groups", "dp")), P(("groups", "dp"), None), P(("groups", "dp"), None, None))
    return jax.shard_map(shards, mesh=mesh, in_specs=in_specs, out_specs=out_specs, check_vma=False)
```

time: 194 us -> 42.3 us (0.22)
  blocking collectives: 158 us -> 0 us
  Pallas kernels: 0 us -> 35.8 us
  other arithmetic: 16 us -> 0 us
  starting transfers between devices: 6.23 us -> 0 us
  matrix products: 4.13 us -> 0 us
    all_gather x1 -> x0, blocking collectives: 96.7 us -> none  [shards(): lax.all_gather(normed, 'dp', axis=0, tiled=True)]
    unnamed x1 -> x0, blocking collectives: 61.2 us -> none
    pallas_call x0 -> x1, Pallas kernels: none -> 35.8 us  [shards(): pl.pallas_call(lambda *refs: kernel(n, per, *refs), out_shape=(jax.ShapeD...]
    concatenate x1 -> x0, other arithmetic: 10.1 us -> none  [extended(): x = jnp.concatenate([before, x, after], axis=dim)]
    ppermute x2 -> x0, starting transfers between devices: 6.23 us -> none  [the longest x1 4.94 us: extended(): before = lax.ppermute(last, axis, up)]
    gather x2 -> x0, local copies, waits for them, and re-layouts: 5.68 us -> none  [the longest x1 5.02 us: shards(): moved_rows = jnp.take(window, chosen, axis=0)]
    dot_general x1 -> x0, matrix products: 4.13 us -> none  [shards(): jnp.dot(lax.all_gather(normed, 'dp', axis=0, tiled=True), exit_weight, pr...]
    slice x3 -> x2, local copies, waits for them, and re-layouts: 0.01 us -> 2.63 us  [shards(): return (valid[:, 127], valid[:, :BINS], moved)]
  transfers between devices with their start and end apart: 2 -> 0, of which waited for: 0 -> 0; matrix products, arithmetic and copies ran while one was open for 6% -> 0% of each run, Pallas kernels for 0% -> 0%
where the time goes in v1:
time: 42.3 us; the launch traced here: 42 us
  Pallas kernels  35.8 us (85%)
  local copies, waits for them, and re-layouts  5.57 us (13%)
  between operations  0.64 us (2%)
    pallas_call x1, Pallas kernels, shards(): pl.pallas_call(lambda *refs: kernel(n, per, *refs), out_shape=(jax.ShapeD...  35.8 us
    unnamed x1, local copies, waits for them, and re-layouts  2.94 us
    slice x2, local copies, waits for them, and re-layouts, shards(): return (valid[:, 127], valid[:, :BINS], moved)  2.63 us

profile of v1, /device:TPU:0, one launch (start us, length us, event | category | flops | bytes accessed | tf_op | source)
XLA Modules:
  0.0 42.0 jit_solution(11350240982367985881)
XLA Ops:
  0.6 35.8 %shard_map.85 = (bf16[2,96,5120]{2,1,0:T(8,128)(2,1)}, f32[8,128]{1,0:T(8,128)}) custom-call(bf16[4,96,5120]{2,1,0:T(8,128)(2,1)} %refs_0_.1, bf16[5120,640]{1,0:T(8,128)(2,1)} %refs_1_.1, f32[1,5120]{1,0:T(1,128)} %bitcast.2, s32[1,64]{1,0:T(1,128)} %bitcast.3, s32[32]{0:T(128)} %refs_4_.1, s32[64]{0:T(128)} %refs_5_.1), custom_call_target="tpu_custom_call" | custom-call | tf_op jit(solution)/shard_map/pallas_call | solution.py:339
  36.5 1.3 %slice.10 = f32[4,15]{1,0:T(4,128)} slice(f32[8,128]{1,0:T(8,128)} %get-tuple-element.5), slice={[4:8], [0:15]} | slice | bytes 480 | tf_op jit(solution)/shard_map/slice | solution.py:379
  37.7 1.4 %slice_reduce_fusion = f32[4]{0:T(128)} fusion(f32[8,128]{1,0:T(8,128)} %get-tuple-element.5), kind=kLoop, calls=%fused_computation | loop fusion | bytes 32 | tf_op jit(solution)/shard_map/slice | solution.py:379
  39.1 2.9 %copy.10 = bf16[2,96,5120]{2,1,0:T(8,128)(2,1)} copy(bf16[2,96,5120]{2,1,0:T(8,128)(2,1)} %get-tuple-element.12) | data formatting | bytes 3932160

commit v2 on v1

--- a/solution.py
+++ b/solution.py
@@ -12,18 +12,12 @@
 EPSILON = 1e-06
 PACK = 16
 CHUNK = 16
+LATER = 1
 MESH = pl.DeviceIdType.MESH
 
 
 def partner_of(me, bit):
     return me + (1 - 2 * ((me // (1 << bit)) % 2)) * (1 << bit)
-
-
-def block_of(me, mask, bits):
-    for bit in range(bits):
-        if mask >> bit & 1:
-            me = partner_of(me, bit)
-    return me
 
 
 def kernel(
@@ -43,7 +37,6 @@
     rows,
     outgoing,
     incoming,
-    staged,
     stats,
     arrived,
     load_sem,
@@ -54,10 +47,8 @@
     big_recv,
     stat_send,
     stat_recv,
-    out_sem,
 ):
     me = lax.axis_index("dp")
-    bits = n.bit_length() - 1
     parts = PACK // per
     width = hidden.shape[2] // parts
     pieces = len(held)
@@ -100,51 +91,66 @@
     gains = jnp.zeros((PACK, width), jnp.float32)
     for q in range(parts):
         gains = jnp.where(part_of == q, gain[:, q * width : (q + 1) * width], gains)
-    rows[me] = (values * scale * gains).astype(jnp.bfloat16)
+    rows[me // 4, (me // 2) % 2, me % 2] = (values * scale * gains).astype(jnp.bfloat16)
 
     pl.semaphore_wait(barrier, n - 1)
 
-    bit_order = list(range(1, bits)) + [0]
-    sent = []
-
-    def send_stage(stage, have):
-        bit = bit_order[stage]
-        new = []
-        for mask in have:
-            j = block_of(me, mask, bits)
-            to = mask ^ (1 << bit)
-            if mask:
-                got(mask)
-            copy = pltpu.make_async_remote_copy(
-                src_ref=rows.at[j],
-                dst_ref=rows.at[j],
-                send_sem=row_send.at[to],
-                recv_sem=row_recv.at[to],
-                device_id={"dp": partner_of(me, bit)},
-                device_id_type=MESH,
-            )
-            copy.start()
-            sent.append(copy)
-            new.append(to)
-        return have + new
-
-    seen = set()
-
-    def got(mask):
-        if mask in seen:
-            return
-        seen.add(mask)
-        j = block_of(me, mask, bits)
-        pltpu.make_async_remote_copy(
-            src_ref=rows.at[j],
-            dst_ref=rows.at[j],
-            send_sem=row_send.at[mask],
-            recv_sem=row_recv.at[mask],
-            device_id={"dp": partner_of(me, 0)},
+    layers = n // 4
+    layer, core = me // 4, me % 2
+    top = layers - 1
+
+    def row_copy(ref, sem, other):
+        return pltpu.make_async_remote_copy(
+            src_ref=ref,
+            dst_ref=ref,
+            send_sem=row_send.at[sem],
+            recv_sem=row_recv.at[sem],
+            device_id={"dp": other},
             device_id_type=MESH,
-        ).wait_recv()
-
-    have = send_stage(0, [0])
+        )
+
+    my_y = (me // 2) % 2
+    ys = (my_y, 1 - my_y)
+    both = range(2)
+
+    def along_y(b):
+        return row_copy(rows.at[layer, ys[b], core], 0, partner_of(me, 1))
+
+    def upward(unit, step, b):
+        other = jnp.minimum(me + 4, n - 4 + me % 4)
+        return row_copy(rows.at[unit, ys[b], core], 1 + 2 * step + b, other)
+
+    def downward(unit, step, b):
+        other = jnp.maximum(me - 4, me % 4)
+        return row_copy(rows.at[unit, ys[b], core], 1 + 2 * top + 2 * step + b, other)
+
+    def across(unit, side, slot, b):
+        sem = 1 + 4 * top + 2 * slot + b
+        return row_copy(rows.at[unit, ys[b], side], sem, partner_of(me, 0))
+
+    def launch(step, b):
+        @pl.when((layer >= step) & (layer < top))
+        def _():
+            upward(layer - step, step, b).start()
+
+        @pl.when((layer + step <= top) & (layer > 0))
+        def _():
+            downward(layer + step, step, b).start()
+
+    def take(step, b):
+        @pl.when(layer - 1 - step >= 0)
+        def _():
+            upward(layer - 1 - step, step, b).wait_recv()
+            across(layer - 1 - step, core, 1 + step, b).start()
+
+        @pl.when(layer + 1 + step <= top)
+        def _():
+            downward(layer + 1 + step, step, b).wait_recv()
+            across(layer + 1 + step, core, top + 1 + step, b).start()
+
+    along_y(0).start()
+    launch(0, 0)
+    across(layer, core, 0, 0).start()
 
     target = [destination[me * per + i] for i in range(per)]
     to_right = jnp.int32(0)
@@ -154,6 +160,8 @@
         to_left = jnp.where(target[i] == me - 1, i, to_left)
     chosen = (to_right, to_left)
     can_send = (me < n - 1, me > 0)
+    far = (me % 4 == 3, me % 4 == 0)
+    near = (me % 4 != 3, me % 4 != 0)
     can_receive = (me > 0, me < n - 1)
 
     def big_copy(side, c):
@@ -173,12 +181,25 @@
         for side in range(2):
             outgoing[side, c] = held[c][chosen[side]]
 
-            @pl.when(can_send[side])
+            @pl.when(can_send[side] & near[side])
             def _():
                 big_copy(side, c).start()
 
-    for stage in range(1, bits):
-        have = send_stage(stage, have)
+    along_y(1).wait_recv()
+    launch(0, 1)
+    across(layer, core, 0, 1).start()
+    for step in range(top):
+        for b in both:
+            take(step, b)
+            if step + 1 < top:
+                launch(step + 1, b)
+        if step == min(LATER, top - 1):
+            for c in order:
+                for side in range(2):
+
+                    @pl.when(can_send[side] & far[side])
+                    def _():
+                        big_copy(side, c).start()
 
     count = exit_ids.shape[0]
 
@@ -204,14 +225,24 @@
     from_right = jnp.where(me < n - 1, from_right, 0)
 
     weight_copy.wait()
-    for mask in range(1, n):
-        got(mask)
+    for b in both:
+        across(layer, 1 - core, 0, b).wait_recv()
+        for step in range(top):
+
+            @pl.when(layer - 1 - step >= 0)
+            def _():
+                across(layer - 1 - step, 1 - core, 1 + step, b).wait_recv()
+
+            @pl.when(layer + 1 + step <= top)
+            def _():
+                across(layer + 1 + step, 1 - core, top + 1 + step, b).wait_recv()
+
     group = min(n, 16)
     high = group * PACK
     every = label_row.shape[1]
 
     def block(b, carry):
-        held_rows = rows[pl.ds(b * group, group)].reshape(high, width)
+        held_rows = rows[pl.ds(b * (group // 4), group // 4)].reshape(high, width)
         row_id = lax.broadcasted_iota(jnp.int32, (high, vocab), 0)
         row_part = (row_id // per) % parts
         logits = jnp.zeros((high, vocab), jnp.float32)
@@ -278,12 +309,9 @@
                 big_copy(side, c).wait_recv()
 
             own = held[c][keeps[side]]
-            staged[side, c] = jnp.where(gets[side] > 0, incoming[side, c], own)
-            pltpu.make_async_copy(
-                staged.at[side, c],
-                moved.at[side, pl.ds(c * CHUNK, CHUNK), :],
-                out_sem.at[side, c],
-            ).start()
+            moved[side, c * CHUNK : (c + 1) * CHUNK, :] = jnp.where(
+                gets[side] > 0, incoming[side, c], own
+            )
 
     def stat_wait(k, carry):
         stat_copy(k, (me + n - k) % n).wait_recv()
@@ -301,28 +329,56 @@
     lane = lax.broadcasted_iota(jnp.int32, (8, 128), 1)
     centre = lane.astype(jnp.float32) + 0.5
     bins = jnp.maximum(0.0, 1.0 - jnp.abs(place - centre))
-    result[...] = jnp.where(lane < BINS, bins, nll)
+    result[0:8, :] = bins
+    row = lax.broadcasted_iota(jnp.int32, (8, 128), 0)
+    nll_row = jnp.sum(jnp.where(lane == row - (8 - per), nll, 0.0), axis=0, keepdims=True)
+    result[8:16, :] = jnp.broadcast_to(nll_row, (8, 128))
 
     for c in order:
         for side in range(2):
-            pltpu.make_async_copy(
-                staged.at[side, c],
-                moved.at[side, pl.ds(c * CHUNK, CHUNK), :],
-                out_sem.at[side, c],
-            ).wait()
 
             @pl.when(can_send[side])
             def _():
                 big_copy(side, c).wait_send()
 
-    for copy in sent:
-        copy.wait_send()
+    along_y(0).wait_send()
+    for b in both:
+        across(layer, core, 0, b).wait_send()
+        for step in range(top):
+
+            @pl.when((layer >= step) & (layer < top))
+            def _():
+                upward(layer - step, step, b).wait_send()
+
+            @pl.when((layer + step <= top) & (layer > 0))
+            def _():
+                downward(layer + step, step, b).wait_send()
+
+            @pl.when(layer - 1 - step >= 0)
+            def _():
+                across(layer - 1 - step, core, 1 + step, b).wait_send()
+
+            @pl.when(layer + 1 + step <= top)
+            def _():
+                across(layer + 1 + step, core, top + 1 + step, b).wait_send()
 
     def stat_done(k, carry):
         stat_copy(k, me).wait_send()
         return carry
 
     lax.fori_loop(1, n, stat_done, 0)
+
+
+def finish(moved, result, nll, bins, out, sems):
+    copies = []
+    for k in range(sems.shape[0]):
+        copies.append(pltpu.make_async_copy(moved.at[k], out.at[k], sems.at[k]))
+        copies[-1].start()
+    per = bins.shape[0]
+    nll[...] = result[8:9, 0:per]
+    bins[...] = result[8 - per : 8, 0:BINS]
+    for copy in copies:
+        copy.wait()
 
 
 def shards(hidden, exit_gain, exit_weight, labels, exit_ids, destination):
@@ -333,36 +389,35 @@
     slots = per // 2
     width = depth // (PACK // per)
     hbm = pl.BlockSpec(memory_space=pl.ANY)
+    pinned = pl.BlockSpec(memory_space=pltpu.HBM)
     vmem = pl.BlockSpec(memory_space=pltpu.VMEM)
     smem = pl.BlockSpec(memory_space=pltpu.SMEM)
     bf16 = jnp.bfloat16
     moved, result = pl.pallas_call(
         lambda *refs: kernel(n, per, *refs),
         out_shape=(
-            jax.ShapeDtypeStruct((slots, length, depth), bf16),
-            jax.ShapeDtypeStruct((8, 128), jnp.float32),
+            pltpu.VMEM((slots, length, depth), bf16),
+            pltpu.VMEM((16, 128), jnp.float32),
         ),
-        in_specs=[hbm, hbm, vmem, vmem, smem, smem],
-        out_specs=(hbm, vmem),
+        in_specs=[pinned, pinned, vmem, vmem, smem, smem],
+        out_specs=(vmem, vmem),
         scratch_shapes=[
             [pltpu.VMEM((per, CHUNK, depth), bf16) for _ in range(pieces)],
             pltpu.VMEM((depth, vocab), bf16),
             pltpu.VMEM((PACK, width), jnp.float32),
-            pltpu.VMEM((n, PACK, width), bf16),
-            pltpu.VMEM((2, pieces, CHUNK, depth), bf16),
+            pltpu.VMEM((n // 4, 2, 2, PACK, width), bf16),
             pltpu.VMEM((2, pieces, CHUNK, depth), bf16),
             pltpu.VMEM((2, pieces, CHUNK, depth), bf16),
             pltpu.VMEM((n, 8, 128), jnp.float32),
             pltpu.VMEM((n, 8, 128), jnp.float32),
             pltpu.SemaphoreType.DMA((pieces,)),
             pltpu.SemaphoreType.DMA,
-            pltpu.SemaphoreType.DMA((n,)),
-            pltpu.SemaphoreType.DMA((n,)),
+            pltpu.SemaphoreType.DMA((2 * n,)),
+            pltpu.SemaphoreType.DMA((2 * n,)),
             pltpu.SemaphoreType.DMA((2, pieces)),
             pltpu.SemaphoreType.DMA((2, pieces)),
             pltpu.SemaphoreType.DMA((n,)),
             pltpu.SemaphoreType.DMA((n,)),
-            pltpu.SemaphoreType.DMA((2, pieces)),
         ],
         compiler_params=pltpu.CompilerParams(
             collective_id=0, has_side_effects=True, vmem_limit_bytes=56 * 1024 * 1024
@@ -375,8 +430,19 @@
         exit_ids,
         destination,
     )
-    valid = result[8 - per :]
-    return valid[:, 127], valid[:, :BINS], moved
+    nll, bins, placed = pl.pallas_call(
+        finish,
+        out_shape=(
+            jax.ShapeDtypeStruct((1, per), jnp.float32),
+            jax.ShapeDtypeStruct((per, BINS), jnp.float32),
+            jax.ShapeDtypeStruct((slots, length, depth), bf16),
+        ),
+        in_specs=[hbm, vmem],
+        out_specs=(vmem, vmem, hbm),
+        scratch_shapes=[pltpu.SemaphoreType.DMA((slots,))],
+        compiler_params=pltpu.CompilerParams(vmem_limit_bytes=2 * 1024 * 1024),
+    )(moved, result)
+    return nll.reshape(per), bins, placed
 
 
 def solution(mesh):

time: 42.3 us -> 34.3 us (0.81)
  local copies, waits for them, and re-layouts: 5.57 us -> 0 us
  Pallas kernels: 35.8 us -> 33.5 us
    unnamed x1 -> x0, local copies, waits for them, and re-layouts: 2.94 us -> none
    slice x2 -> x0, local copies, waits for them, and re-layouts: 2.63 us -> none  [shards(): return (valid[:, 127], valid[:, :BINS], moved)]
    pallas_call x1 -> x2, Pallas kernels: 35.8 us -> 33.5 us  [the longest x1 31.7 us: shards(): pl.pallas_call(lambda *refs: kernel(n, per, *refs), out_shape=(pltpu.VMEM...]
where the time goes in v2:
time: 34.3 us; the launch traced here: 34.2 us
  Pallas kernels  33.5 us (98%)
  between operations  0.64 us (2%)
    pallas_call x1, Pallas kernels, shards(): pl.pallas_call(lambda *refs: kernel(n, per, *refs), out_shape=(pltpu.VMEM...  31.7 us
    pallas_call x1, Pallas kernels, shards(): pl.pallas_call(finish, out_shape=(jax.ShapeDtypeStruct((1, per), jnp.floa...  1.87 us

profile of v2, /device:TPU:0, one launch (start us, length us, event | category | flops | bytes accessed | tf_op | source)
XLA Modules:
  0.0 34.2 jit_solution(7854932208424098049)
XLA Ops:
  0.6 31.7 %shard_map.85 = (bf16[2,96,5120]{2,1,0:T(8,128)(2,1)S(1)}, f32[16,128]{1,0:T(8,128)S(1)}) custom-call(bf16[4,96,5120]{2,1,0:T(8,128)(2,1)} %refs_0_.1, bf16[5120,640]{1,0:T(8,128)(2,1)} %refs_1_.1, f32[1,5120]{1,0:T(1,128)} %bitcast.3, s32[1,64]{1,0:T(1,128)} %bitcast.4, s32[32]{0:T(128)} %refs_4_.1, s32[64]{0:T(128)} %refs_5_.1), custom_call_target="tpu_custom_call" | custom-call | tf_op jit(solution)/shard_map/pallas_call | solution.py:396
  32.3 1.9 %shard_map.86 = (f32[1,4]{1,0:T(1,128)}, f32[4,15]{1,0:T(4,128)}, bf16[2,96,5120]{2,1,0:T(8,128)(2,1)}) custom-call(bf16[2,96,5120]{2,1,0:T(8,128)(2,1)S(1)} %get-tuple-element.8.moved, f32[16,128]{1,0:T(8,128)S(1)} %get-tuple-element.9.result), custom_call_target="tpu_custom_call" | custom-call | tf_op jit(solution)/shard_map/pallas_call | solution.py:433

commit v3 on v2

--- a/solution.py
+++ b/solution.py
@@ -11,7 +11,7 @@
 BINS = 15
 EPSILON = 1e-06
 PACK = 16
-CHUNK = 16
+CHUNK = 32
 LATER = 1
 MESH = pl.DeviceIdType.MESH
 

time: 34.3 us -> 34.2 us (level)
  no operation moved by 1% of the time
where the time goes in v3:
time: 34.2 us; the launch traced here: 34 us
  Pallas kernels  33.4 us (98%)
  between operations  0.64 us (2%)
    pallas_call x1, Pallas kernels, shards(): pl.pallas_call(lambda *refs: kernel(n, per, *refs), out_shape=(pltpu.VMEM...  31.5 us
    pallas_call x1, Pallas kernels, shards(): pl.pallas_call(finish, out_shape=(jax.ShapeDtypeStruct((1, per), jnp.floa...  1.87 us

profile of v3, /device:TPU:0, one launch (start us, length us, event | category | flops | bytes accessed | tf_op | source)
XLA Modules:
  0.0 34.0 jit_solution(3910132275107135020)
XLA Ops:
  0.6 31.5 %shard_map.85 = (bf16[2,96,5120]{2,1,0:T(8,128)(2,1)S(1)}, f32[16,128]{1,0:T(8,128)S(1)}) custom-call(bf16[4,96,5120]{2,1,0:T(8,128)(2,1)} %refs_0_.1, bf16[5120,640]{1,0:T(8,128)(2,1)} %refs_1_.1, f32[1,5120]{1,0:T(1,128)} %bitcast.3, s32[1,64]{1,0:T(1,128)} %bitcast.4, s32[32]{0:T(128)} %refs_4_.1, s32[64]{0:T(128)} %refs_5_.1), custom_call_target="tpu_custom_call" | custom-call | tf_op jit(solution)/shard_map/pallas_call | solution.py:396
  32.2 1.9 %shard_map.86 = (f32[1,4]{1,0:T(1,128)}, f32[4,15]{1,0:T(4,128)}, bf16[2,96,5120]{2,1,0:T(8,128)(2,1)}) custom-call(bf16[2,96,5120]{2,1,0:T(8,128)(2,1)S(1)} %get-tuple-element.8.moved, f32[16,128]{1,0:T(8,128)S(1)} %get-tuple-element.9.result), custom_call_target="tpu_custom_call" | custom-call | tf_op jit(solution)/shard_map/pallas_call | solution.py:433
